TPU v7x, 32 devices: a whole 2x2x4 slice. The times are simulated.
32 devices in a mesh: xy: 8 (over y, x, core), gz: 4 (over z).
Axes of the slice: x: 2, y: 2, z: 4, core: 2. Of those that a mesh axis runs over, the one named last changes fastest.
Arguments:
- electric: float32 [4, 2048, 2048], P('gz', 'xy'), may hold values from -6 to 6
- magnetic_first: float32 [4, 2048, 2048], P('gz', 'xy'), may hold values from -6 to 6
- magnetic_second: float32 [4, 2048, 2048], P('gz', 'xy'), may hold values from -6 to 6
- region: int32 [4, 2048, 2048], P('gz', 'xy'), may hold values from 0 to 7
- permittivity_table: float32 [8], replicated, may hold values from 1 to 12
- conductivity_table: float32 [8], replicated, may hold values from 0.02 to 4
Outputs:
- electric_final: float32 [4, 2048, 2048], P('gz', 'xy')
- first_final: float32 [4, 2048, 2048], P('gz', 'xy')
- second_final: float32 [4, 2048, 2048], P('gz', 'xy')
All inputs are finite; a program needn't handle non-finite values.
Results may differ from a plain program's by a relative error of at most 0.000024.
Values sent between devices are 32-bit elements; how exact they have to be, the bound alone decides.
A program may use at most 128 MiB of HBM per device.

v0:
```python
import functools

import jax
import jax.numpy as jnp
from jax import lax
from jax.experimental import pallas as pl
from jax.experimental.pallas import tpu as pltpu
from jax.sharding import PartitionSpec as P

time_step = 4.0
vertical_coupling = 0.5
run_length = 32
vmem_bytes = 56 * 1024 * 1024


def passed_along(value, axis, steps):
    count = lax.axis_size(axis)
    initial, last = (max(0, -steps), min(count, count - steps))
    return lax.ppermute(value, axis, [(source, source + steps) for source in range(initial, last)])


def shifted(values, step, axis):
    size = values.shape[axis]
    return pltpu.roll(values, step % size, axis)


def row_index(shape):
    return lax.broadcasted_iota(jnp.int32, shape, 0)


def lookup(region, entries):
    level = list(entries)
    bit = 1
    while len(level) > 1:
        on = (region & bit) != 0
        level = [jnp.where(on, level[i + 1], level[i]) for i in range(0, len(level), 2)]
        bit *= 2
    return level[0]


def cyclic(diagonal, lower, upper, right_side):
    count = diagonal.shape[0]
    stride = 1
    while stride < count:
        inverse = 1.0 / diagonal
        alpha = lower * shifted(inverse, stride, 0)
        beta = upper * shifted(inverse, -stride, 0)
        diagonal = (
            diagonal
            - alpha * shifted(upper, stride, 0)
            - beta * shifted(lower, -stride, 0)
        )
        right_side = (
            right_side
            + alpha * shifted(right_side, stride, 0)
            + beta * shifted(right_side, -stride, 0)
        )
        lower = alpha * shifted(lower, stride, 0)
        upper = beta * shifted(upper, -stride, 0)
        stride *= 2
    return right_side / diagonal


def run_rows(ref, step, runs, length):
    return ref[pl.ds(step, runs, stride=length), :]


def run_blocks(ref, blocks, step, runs, length):
    return jnp.concatenate(
        [ref[block, pl.ds(step, runs, stride=length), :] for block in blocks], axis=1
    )


def eliminate(diagonal_of, right_of, runs, length, c_ref, g_ref, f_ref):
    c = g = f = total_g = total_f = None
    for i in range(length - 1):
        d, b = diagonal_of(i), right_of(i)
        if i == 0:
            inverse = 1.0 / d
            c = time_step * inverse
            g = b * inverse
            f = c
            total_g, total_f = g, f
        else:
            inverse = 1.0 / (d - time_step * c)
            c = time_step * inverse
            g = (b + time_step * g) * inverse
            before = f
            f = c * f
            total_g = total_g + before * g
            total_f = total_f + before * f
        rows = pl.ds(i * runs, runs)
        c_ref[rows, :] = c
        g_ref[rows, :] = g
        f_ref[rows, :] = f
    d, b = diagonal_of(length - 1), right_of(length - 1)
    return (
        d - time_step * c,
        b + time_step * g,
        time_step * f,
        time_step * total_g,
        time_step * total_f,
    )


def back(last, before, runs, length, c_ref, g_ref, f_ref, put):
    x = last
    put(length - 1, x)
    for i in range(length - 2, -1, -1):
        rows = pl.ds(i * runs, runs)
        x = g_ref[rows, :] + c_ref[rows, :] * x + f_ref[rows, :] * before
        put(i, x)


def table_entries(eps_ref, sig_ref):
    eps = [eps_ref[k] / time_step for k in range(eps_ref.shape[0])]
    sig = [0.5 * sig_ref[k] for k in range(sig_ref.shape[0])]
    return [a + b for a, b in zip(eps, sig)], [a - b for a, b in zip(eps, sig)]


def column_block(block, parts):
    return block % parts, slice((block // parts) * 128, (block // parts) * 128 + 128)


def x_kernel(parts, e_ref, up_ref, down_ref, hx_ref, hx_edge_ref, hy_ref, region_ref,
             eps_ref, sig_ref, *rest):
    outs, (rhs, dia, rhs_t, dia_t, c_ref, g_ref, f_ref) = rest[:parts], rest[parts:]
    rows, columns = e_ref.shape
    plus, minus = table_entries(eps_ref, sig_ref)
    for first in range(0, rows, 8):
        here = pl.ds(first, 8)
        e, hx, hy, region = e_ref[here, :], hx_ref[here, :], hy_ref[here, :], region_ref[here, :]
        column = lax.broadcasted_iota(jnp.int32, e.shape, 1)
        edge = hx_edge_ref[0:1, :] if first == 0 else hx_ref[first - 1:first, :]
        hx_before = jnp.where(row_index(e.shape) == 0, edge, shifted(hx, 1, 0))
        hy_before = jnp.where(column == 0, 0.0, shifted(hy, 1, 1))
        layer = up_ref[here, :] + down_ref[here, :] - 2.0 * e
        rhs[here, :] = (
            lookup(region, minus) * e
            + (hy - hy_before)
            - (hx - hx_before)
            + vertical_coupling * layer
        )
        dia[here, :] = lookup(region, plus) + jnp.where(column == 0, time_step, 2.0 * time_step)
    if rhs.shape[0] > rows:
        rest_shape = (rhs.shape[0] - rows, columns)
        rhs[rows:, :] = jnp.zeros(rest_shape, jnp.float32)
        dia[rows:, :] = jnp.full(rest_shape, 3.0 * time_step, jnp.float32)
    for start in range(0, columns, 128):
        rhs_t[start:start + 128, :] = rhs[:, start:start + 128].T
        dia_t[start:start + 128, :] = dia[:, start:start + 128].T
    runs, length = columns // run_length, run_length
    d, b, off, part_g, part_f = eliminate(
        lambda i: run_rows(dia_t, i, runs, length),
        lambda i: run_rows(rhs_t, i, runs, length),
        runs, length, c_ref, g_ref, f_ref,
    )
    place = row_index(d.shape)
    off = jnp.where(place == 0, 0.0, off)
    end = place == runs - 1
    d = d - jnp.where(end, 0.0, shifted(part_f, -1, 0))
    b = b + jnp.where(end, 0.0, shifted(part_g, -1, 0))
    solved = cyclic(d, off, jnp.where(end, 0.0, shifted(off, -1, 0)), b)
    before = jnp.where(place == 0, 0.0, shifted(solved, 1, 0))

    def put(i, x):
        rhs_t[pl.ds(i, runs, stride=length), :] = x

    back(solved, before, runs, length, c_ref, g_ref, f_ref, put)
    for block in range(columns // 128):
        part, place = column_block(block, parts)
        outs[part][:, place] = rhs_t[block * 128:block * 128 + 128, :].T[:rows]


def middle_kernel(parts, pieces, first_ref, e_ref, hx_ref, hy_ref, region_ref, e_before_ref,
                  e_after_ref, hx_edge_ref, eps_ref, sig_ref, *rest):
    halves = rest[:parts * pieces]
    rhs_outs = rest[parts * pieces:parts * pieces + parts]
    dia_outs = rest[parts * pieces + parts:parts * pieces + 2 * parts]
    hx_outs = rest[parts * pieces + 2 * parts:parts * pieces + 3 * parts]
    hy_out, half_ref, full_ref = rest[parts * pieces + 3 * parts:]
    rows, columns = e_ref.shape
    piece_rows = rows // pieces
    blocks = columns // 128
    for piece in range(pieces):
        for block in range(blocks):
            part, place = column_block(block, parts)
            half_ref[piece * piece_rows:(piece + 1) * piece_rows, block * 128:block * 128 + 128] = (
                halves[piece * parts + part][:, place]
            )
    plus, minus = table_entries(eps_ref, sig_ref)
    edge_before = hx_edge_ref[0:1, :] - time_step * (e_ref[0:1, :] - e_before_ref[0:1, :])
    edge_before = jnp.where(first_ref[0] > 0, 0.0, edge_before)
    for first in range(0, rows, 8):
        here = pl.ds(first, 8)
        e, hx, hy, region = e_ref[here, :], hx_ref[here, :], hy_ref[here, :], region_ref[here, :]
        half = half_ref[here, :]
        place = row_index(e.shape)
        column = lax.broadcasted_iota(jnp.int32, e.shape, 1)
        after = e_after_ref[0:1, :] if first + 8 == rows else e_ref[first + 8:first + 9, :]
        e_after = jnp.where(place == 7, after, shifted(e, -1, 0))
        half_hx = hx - time_step * (e_after - e)
        hx_before = jnp.where(place == 0, edge_before, shifted(half_hx, 1, 0))
        edge_before = half_hx[7:8, :]
        half_after = jnp.where(column == columns - 1, 0.0, shifted(half, -1, 1))
        change = time_step * (half_after - half)
        half_hy = hy + change
        full_ref[here, :] = half_hy + change
        hy_before = jnp.where(column == 0, 0.0, shifted(half_hy, 1, 1))
        right_side = (
            lookup(region, minus) * half
            + (half_hy - hy_before)
            - (half_hx - hx_before)
            - (2.0 * vertical_coupling) * half
        )
        ramp = 2.0 * time_step
        diagonal = lookup(region, plus) + ramp
        if first == 0:
            start = jnp.where(first_ref[0] > 0, time_step, 2.0 * time_step)
            diagonal = lookup(region, plus) + jnp.where(place == 0, start, ramp)
        for block in range(blocks):
            part, spot = column_block(block, parts)
            source = slice(block * 128, block * 128 + 128)
            rhs_outs[part][here, spot] = right_side[:, source]
            dia_outs[part][spot.start // 128, here, :] = diagonal[:, source]
            hx_outs[part][here, spot] = half_hx[:, source]
    for block in range(blocks):
        hy_out[block * 128:block * 128 + 128, :] = full_ref[:, block * 128:block * 128 + 128].T


def y_first_kernel(pieces, runs, rhs_ref, dia_ref, *rest):
    ups, downs = rest[:pieces], rest[pieces:2 * pieces]
    c_ref, g_ref, f_ref, second_ref, sent_ref, total = rest[2 * pieces:]
    rows, columns = rhs_ref.shape
    piece_rows = rows // pieces
    for piece in range(pieces):
        here = slice(piece * piece_rows, (piece + 1) * piece_rows)
        for block in range(columns // 128):
            spot = slice(block * 128, block * 128 + 128)
            total[block, here, :] = rhs_ref[here, spot] + vertical_coupling * (
                ups[piece][:, spot] + downs[piece][:, spot]
            )
    length = rows // runs
    for start in range(0, columns, 512):
        some = pl.ds(start, 512)
        blocks = range(start // 128, start // 128 + 4)
        d, b, off, part_g, part_f = eliminate(
            lambda i: run_blocks(dia_ref, blocks, i, runs, length),
            lambda i: run_blocks(total, blocks, i, runs, length),
            runs, length, c_ref.at[:, some], g_ref.at[:, some], f_ref.at[:, some],
        )
        end = row_index(d.shape) == runs - 1
        d = d - jnp.where(end, 0.0, shifted(part_f, -1, 0))
        b = b + jnp.where(end, 0.0, shifted(part_g, -1, 0))
        coupling = [off[k:k + 1, :] for k in range(runs)]
        c = g = f = total_g = total_f = factor = None
        for k in range(runs - 1):
            if k == 0:
                inverse = 1.0 / d[0:1, :]
                c = coupling[1] * inverse
                g = b[0:1, :] * inverse
                f = coupling[0] * inverse
                total_g, total_f, factor = g, f, c
            else:
                inverse = 1.0 / (d[k:k + 1, :] - coupling[k] * c)
                c = coupling[k + 1] * inverse
                g = (b[k:k + 1, :] + coupling[k] * g) * inverse
                f = coupling[k] * f * inverse
                total_g = total_g + factor * g
                total_f = total_f + factor * f
                factor = factor * c
            second_ref[k:k + 1, some] = c
            second_ref[runs + k:runs + k + 1, some] = g
            second_ref[2 * runs + k:2 * runs + k + 1, some] = f
        sent_ref[0:1, some] = d[runs - 1:runs, :] - coupling[runs - 1] * c
        sent_ref[1:2, some] = b[runs - 1:runs, :] + coupling[runs - 1] * g
        sent_ref[2:3, some] = coupling[runs - 1] * f
        sent_ref[3:4, some] = part_g[0:1, :] + coupling[0] * total_g
        sent_ref[4:5, some] = part_f[0:1, :] + coupling[0] * total_f
        sent_ref[5:8, some] = jnp.zeros((3, 512), jnp.float32)


def y_second_kernel(count, runs, me_ref, all_ref, c_ref, g_ref, f_ref, second_ref, hx_ref,
                    e_out, hx_out, e_scr, hx_scr, solved_scr):
    rows, columns = hx_ref.shape
    length = rows // runs
    me = me_ref[0]
    for start in range(0, columns, 512):
        some = pl.ds(start, 512)
        blocks = range(start // 128, start // 128 + 4)
        d, b, off, part_g, part_f = [
            all_ref[q, :, some] for q in range(5)
        ]
        place = row_index(d.shape)
        end = place == count - 1
        off = jnp.where(place == 0, 0.0, off)
        off_next = jnp.where(end, 0.0, shifted(off, -1, 0))
        f_next = jnp.where(end, 0.0, shifted(part_f, -1, 0))
        g_next = jnp.where(end, 0.0, shifted(part_g, -1, 0))
        solved = cyclic(d - f_next, off, off_next, b + g_next)
        next_row = (
            g_next
            + f_next * solved
            + off_next * jnp.where(end, 0.0, shifted(solved, -1, 0))
        ) / time_step

        def row_of(values, index):
            return jnp.sum(jnp.where(place == index, values, 0.0), axis=0, keepdims=True)

        own, previous = row_of(solved, me), row_of(solved, me - 1)
        beyond = row_of(next_row, me)
        value = own
        solved_scr[runs - 1:runs, some] = own
        for k in range(runs - 2, -1, -1):
            value = (
                second_ref[runs + k:runs + k + 1, some]
                + second_ref[k:k + 1, some] * value
                + second_ref[2 * runs + k:2 * runs + k + 1, some] * previous
            )
            solved_scr[k:k + 1, some] = value
        last = solved_scr[:, some]
        before = jnp.where(row_index(last.shape) == 0, previous, shifted(last, 1, 0))

        def put(i, x):
            for n, block in enumerate(blocks):
                e_scr[block, pl.ds(i, runs, stride=length), :] = x[:, n * 128:n * 128 + 128]

        back(last, before, runs, length, c_ref.at[:, some], g_ref.at[:, some],
             f_ref.at[:, some], put)
        for first in range(0, rows, 8):
            here = pl.ds(first, 8)
            e = jnp.concatenate([e_scr[n, here, :] for n in blocks], axis=1)
            after = beyond
            if first + 8 < rows:
                after = jnp.concatenate(
                    [e_scr[n, first + 8:first + 9, :] for n in blocks], axis=1
                )
            e_after = jnp.where(row_index(e.shape) == 7, after, shifted(e, -1, 0))
            hx_scr[here, some] = hx_ref[here, some] - time_step * (e_after - e)
    for start in range(0, columns, 128):
        block = slice(start, start + 128)
        e_out[block, :] = e_scr[start // 128].T
        hx_out[block, :] = hx_scr[:, block].T


in_vmem = pl.BlockSpec(memory_space=pltpu.VMEM)
in_smem = pl.BlockSpec(memory_space=pltpu.SMEM)


def called(kernel, outs, scratch, specs, values, operands):
    return pl.pallas_call(
        kernel,
        out_shape=[jax.ShapeDtypeStruct(shape, jnp.float32) for shape in outs],
        in_specs=specs,
        out_specs=[in_vmem] * len(outs),
        scratch_shapes=[pltpu.VMEM(shape, jnp.float32) for shape in scratch],
        compiler_params=pltpu.CompilerParams(vmem_limit_bytes=vmem_bytes),
        cost_estimate=pl.CostEstimate(
            flops=40 * values, bytes_accessed=30 * values, transcendentals=0
        ),
    )(*operands)


def local(
    electric, magnetic_first, magnetic_second, region, permittivity_table, conductivity_table
):
    count = lax.axis_size("xy")
    me = lax.axis_index("xy")
    _, rows, columns = electric.shape
    width = columns // count
    pieces = 2 if rows % 256 == 0 else 1
    parts = 2 if width == 256 else 1
    piece_rows = rows // pieces
    part_columns = columns // parts
    runs = 8
    electric, hx, hy, region = (
        v.reshape(rows, columns) for v in (electric, magnetic_first, magnetic_second, region)
    )
    eps, sig = permittivity_table, conductivity_table
    first_flag = (me == 0).astype(jnp.int32).reshape(1)
    me_value = me.astype(jnp.int32).reshape(1)

    cut = [slice(p * piece_rows, (p + 1) * piece_rows) for p in range(pieces)]
    ups = [passed_along(electric[c], "gz", 1) for c in cut]
    downs = [passed_along(electric[c], "gz", -1) for c in cut]
    hx_edge = passed_along(hx[-1:], "xy", 1)
    e_before = passed_along(electric[-1:], "xy", 1)
    e_after = passed_along(electric[:1], "xy", -1)

    halves = []
    lines = max(piece_rows, 128)
    t_shape = (columns, lines)
    for p in range(pieces):
        edge = hx_edge if p == 0 else hx[p * piece_rows - 1:p * piece_rows]
        halves.append(called(
            functools.partial(x_kernel, parts),
            [(piece_rows, part_columns)] * parts,
            [(lines, columns)] * 2 + [t_shape] * 2 + [((run_length - 1) * columns // run_length, lines)] * 3,
            [in_vmem] * 7 + [in_smem] * 2,
            piece_rows * columns,
            (electric[cut[p]], ups[p], downs[p], hx[cut[p]], edge, hy[cut[p]], region[cut[p]],
             eps, sig),
        ))
    half_up = [[passed_along(halves[p][c], "gz", 1) for p in range(pieces)] for c in range(parts)]
    half_down = [
        [passed_along(halves[p][c], "gz", -1) for p in range(pieces)] for c in range(parts)
    ]
    middle = called(
        functools.partial(middle_kernel, parts, pieces),
        [(rows, part_columns)] * parts
        + [(part_columns // 128, rows, 128)] * parts
        + [(rows, part_columns)] * parts
        + [(columns, rows)],
        [(rows, columns)] * 2,
        [in_smem] + [in_vmem] * 7 + [in_smem] * 2 + [in_vmem] * (parts * pieces),
        rows * columns,
        (first_flag, electric, hx, hy, region, e_before, e_after, hx_edge, eps, sig,
         *[halves[p][c] for p in range(pieces) for c in range(parts)]),
    )
    right_sides, diagonals = middle[:parts], middle[parts:2 * parts]
    half_hx, full_hy_t = middle[2 * parts:3 * parts], middle[3 * parts]

    def exchanged(values, size):
        moved = lax.all_to_all(
            values.reshape(count, size, rows), "xy", split_axis=0, concat_axis=0, tiled=True
        )
        return moved

    def joined(moved):
        return jnp.transpose(moved, (1, 0, 2)).reshape(1, moved.shape[1], count * rows)

    full_hy = joined(exchanged(full_hy_t, width))
    pairs = []
    for c in range(parts):
        length = rows // runs
        kept = ((length - 1) * runs, part_columns)
        firsts = called(
            functools.partial(y_first_kernel, pieces, runs),
            [kept] * 3 + [(3 * runs, part_columns), (8, part_columns)],
            [(part_columns // 128, rows, 128)],
            [in_vmem] * (2 + 2 * pieces),
            rows * part_columns,
            (right_sides[c], diagonals[c], *half_up[c], *half_down[c]),
        )
        everyone = jnp.swapaxes(lax.all_gather(firsts[4], "xy"), 0, 1)
        seconds = called(
            functools.partial(y_second_kernel, count, runs),
            [(part_columns, rows)] * 2,
            [(part_columns // 128, rows, 128), (rows, part_columns), (runs, part_columns)],
            [in_smem] + [in_vmem] * 6,
            rows * part_columns,
            (me_value, everyone, *firsts[:4], half_hx[c]),
        )
        pairs.append([exchanged(v, width // parts) for v in seconds])
    full_e, full_hx = (
        joined(jnp.concatenate([pair[q] for pair in pairs], axis=1)) for q in range(2)
    )
    return (full_e, full_hx, full_hy)


def solution(mesh):
    in_specs = (
        P("gz", "xy", None),
        P("gz", "xy", None),
        P("gz", "xy", None),
        P("gz", "xy", None),
        P(),
        P(),
    )
    out_specs = (P("gz", "xy", None), P("gz", "xy", None), P("gz", "xy", None))
    return jax.shard_map(local, mesh=mesh, in_specs=in_specs, out_specs=out_specs, check_vma=False)
```

profile of v0, /device:TPU:0, one launch (start us, length us, event | category | flops | bytes accessed | tf_op | source)
XLA Modules:
  0.0 264.8 jit_solution(13489752275791958900)
XLA Ops:
  2.6 5.0 %collective-permute-start.3 = (f32[128,2048]{1,0:T(8,128)S(1)}, f32[128,2048]{1,0:T(8,128)S(1)}, u32[]{:S(2)}, u32[]{:S(2)}) collective-permute-start(f32[128,2048]{1,0:T(8,128)S(1)} %get-tuple-element.62.e_ref), channel_id=1, source_target_pairs={{0,1},{1,2},{2,3},{4,5},{5,6},{6,7},{8,9},{9,10},{10,11},{12,13},{... | collective-permute-start | bytes 3145736 | tf_op jit(solution)/shard_map/ppermute | solution.py:19
  8.9 4.6 %collective-permute-start.5 = (f32[128,2048]{1,0:T(8,128)S(1)}, f32[128,2048]{1,0:T(8,128)S(1)}, u32[]{:S(2)}, u32[]{:S(2)}) collective-permute-start(f32[128,2048]{1,0:T(8,128)S(1)} %get-tuple-element.61.e_ref), channel_id=1, source_target_pairs={{0,1},{1,2},{2,3},{4,5},{5,6},{6,7},{8,9},{9,10},{10,11},{12,13},{... | collective-permute-start | bytes 3145736 | tf_op jit(solution)/shard_map/ppermute | solution.py:19
  20.4 10.6 %collective-permute-done.3.up_ref = f32[128,2048]{1,0:T(8,128)S(1)} collective-permute-done((f32[128,2048]{1,0:T(8,128)S(1)}, f32[128,2048]{1,0:T(8,128)S(1)}, u32[]{:S(2)}, u32[]{:S(2)}) %collective-permute-start.3) | collective-permute-done | bytes 1048608 | tf_op jit(solution)/shard_map/ppermute | solution.py:19
  31.1 4.5 %collective-permute-done.4.down_ref = f32[128,2048]{1,0:T(8,128)S(1)} collective-permute-done((f32[128,2048]{1,0:T(8,128)S(1)}, f32[128,2048]{1,0:T(8,128)S(1)}, u32[]{:S(2)}, u32[]{:S(2)}) %collective-permute-start.4) | collective-permute-done | bytes 1048608 | tf_op jit(solution)/shard_map/ppermute | solution.py:19
  36.5 8.5 %shard_map.85 = (f32[128,1024]{1,0:T(8,128)}, f32[128,1024]{1,0:T(8,128)}) custom-call(f32[128,2048]{1,0:T(8,128)} %copy-done.5, f32[128,2048]{1,0:T(8,128)} %copy-done.10, f32[128,2048]{1,0:T(8,128)} %copy-done.11, f32[128,2048]{1,0:T(8,128)} %get-tuple-element.65.hx_ref, f32[1,2048]{1,0:T(1,128)} %copy-done.22, f32[128,2048]{1,0:T(8,128)} %get-tuple-element.56.hy_ref, ...), custom_call_target="tpu_custom_call" | custom-call | flops 10485760 | bytes 7864320 | tf_op jit(solution)/shard_map/pallas_call | solution.py:351
  53.5 4.5 %collective-permute-done.6.down_ref = f32[128,2048]{1,0:T(8,128)S(1)} collective-permute-done((f32[128,2048]{1,0:T(8,128)S(1)}, f32[128,2048]{1,0:T(8,128)S(1)}, u32[]{:S(2)}, u32[]{:S(2)}) %collective-permute-start.6) | collective-permute-done | bytes 1048608 | tf_op jit(solution)/shard_map/ppermute | solution.py:19
  59.0 8.5 %shard_map.86 = (f32[128,1024]{1,0:T(8,128)}, f32[128,1024]{1,0:T(8,128)}) custom-call(f32[128,2048]{1,0:T(8,128)} %copy-done.4, f32[128,2048]{1,0:T(8,128)} %copy-done.8, f32[128,2048]{1,0:T(8,128)} %copy-done.9, f32[128,2048]{1,0:T(8,128)} %get-tuple-element.66.hx_ref, f32[1,2048]{1,0:T(1,128)} %get-tuple-element.57.hx_edge_ref, ...), custom_call_target="tpu_custom_call" | custom-call | flops 10485760 | bytes 7864320 | tf_op jit(solution)/shard_map/pallas_call | solution.py:351
  68.8 4.6 %collective-permute-start.8 = (f32[128,1024]{1,0:T(8,128)}, f32[128,1024]{1,0:T(8,128)S(1)}, u32[]{:S(2)}, u32[]{:S(2)}) collective-permute-start(f32[128,1024]{1,0:T(8,128)} %get-tuple-element.30.rest_2_), channel_id=1, source_target_pairs={{0,1},{1,2},{2,3},{4,5},{5,6},{6,7},{8,9},{9,10},{10,11},{12,13},{... | collective-permute-start | bytes 1572872 | tf_op jit(solution)/shard_map/ppermute | solution.py:19
  81.7 10.4 %shard_map.87 = (f32[256,1024]{1,0:T(8,128)}, f32[256,1024]{1,0:T(8,128)}, f32[8,256,128]{2,1,0:T(8,128)}, f32[8,256,128]{2,1,0:T(8,128)}, f32[256,1024]{1,0:T(8...) custom-call(s32[1]{0:T(128)} %bitcast.1.first_ref, f32[256,2048]{1,0:T(8,128)} %bitcast.48, f32[256,2048]{1,0:T(8,128)} %bitcast.49, ...), custom_call_target="tpu_custom_call" | custom-call | flops 20971520 | bytes 15728640 | tf_op jit(solution)/shard_map/pallas_call | solution.py:351
  93.5 5.7 %shard_map.88 = (f32[248,1024]{1,0:T(8,128)}, f32[248,1024]{1,0:T(8,128)}, f32[248,1024]{1,0:T(8,128)}, f32[24,1024]{1,0:T(8,128)}, f32[8,1024]{1,0:T(8,128)}) custom-call(f32[256,1024]{1,0:T(8,128)} %get-tuple-element.32.rhs_ref, f32[8,256,128]{2,1,0:T(8,128)} %get-tuple-element.33.dia_ref, f32[128,1024]{1,0:T(8,128)} %copy-done.14, ...), custom_call_target="tpu_custom_call" | custom-call | flops 10485760 | bytes 7864320 | tf_op jit(solution)/shard_map/pallas_call | solution.py:351
  99.2 11.6 %all-gather = f32[64,1024]{1,0:T(8,128)S(1)} all-gather(f32[8,1024]{1,0:T(8,128)} %get-tuple-element.34), channel_id=2, replica_groups=mesh['xy'=8,'gz'=4] {'xy'}, dimensions={0}, use_global_device_ids=true | all-gather | bytes 294912 | tf_op jit(solution)/shard_map/all_gather | solution.py:445
  111.7 4.8 %shard_map.89 = (f32[1024,256]{1,0:T(8,128)}, f32[1024,256]{1,0:T(8,128)}) custom-call(s32[1]{0:T(128)} %bitcast.me_ref, f32[8,8,1024]{2,1,0:T(8,128)} %bitcast.55, f32[248,1024]{1,0:T(8,128)} %get-tuple-element.35.c_ref, f32[248,1024]{1,0:T(8,128)} %get-tuple-element.36.g_ref, f32[248,1024]{1,0:T(8,128)} %get-tuple-element.37.f_ref, ...), custom_call_target="tpu_custom_call" | custom-call | flops 10485760 | bytes 7864320 | tf_op jit(solution)/shard_map/pallas_call | solution.py:351
  125.0 4.6 %collective-permute-start.12 = (f32[128,1024]{1,0:T(8,128)S(1)}, f32[128,1024]{1,0:T(8,128)S(1)}, u32[]{:S(2)}, u32[]{:S(2)}) collective-permute-start(f32[128,1024]{1,0:T(8,128)S(1)} %copy-done.13), channel_id=1, source_target_pairs={{0,1},{1,2},{2,3},{4,5},{5,6},{6,7},{8,9},{9,10},{10,11},{12,13},{... | collective-permute-start | bytes 1572872 | tf_op jit(solution)/shard_map/ppermute | solution.py:19
  130.8 5.0 %collective-permute-done.11.rest_0_ = f32[128,1024]{1,0:T(8,128)S(1)} collective-permute-done((f32[128,1024]{1,0:T(8,128)S(1)}, f32[128,1024]{1,0:T(8,128)S(1)}, u32[]{:S(2)}, u32[]{:S(2)}) %collective-permute-start.11) | collective-permute-done | bytes 524320 | tf_op jit(solution)/shard_map/ppermute | solution.py:19
  135.9 4.5 %collective-permute-done.13.rest_2_ = f32[128,1024]{1,0:T(8,128)S(1)} collective-permute-done((f32[128,1024]{1,0:T(8,128)S(1)}, f32[128,1024]{1,0:T(8,128)S(1)}, u32[]{:S(2)}, u32[]{:S(2)}) %collective-permute-start.13) | collective-permute-done | bytes 524320 | tf_op jit(solution)/shard_map/ppermute | solution.py:19
  140.3 6.2 %collective-permute-done.12.rest_1_ = f32[128,1024]{1,0:T(8,128)S(1)} collective-permute-done((f32[128,1024]{1,0:T(8,128)S(1)}, f32[128,1024]{1,0:T(8,128)S(1)}, u32[]{:S(2)}, u32[]{:S(2)}) %collective-permute-start.12) | collective-permute-done | bytes 524320 | tf_op jit(solution)/shard_map/ppermute | solution.py:19
  146.5 4.1 %collective-permute-done.14.rest_3_ = f32[128,1024]{1,0:T(8,128)S(1)} collective-permute-done((f32[128,1024]{1,0:T(8,128)S(1)}, f32[128,1024]{1,0:T(8,128)S(1)}, u32[]{:S(2)}, u32[]{:S(2)}) %collective-permute-start.14) | collective-permute-done | bytes 524320 | tf_op jit(solution)/shard_map/ppermute | solution.py:19
  151.5 5.7 %shard_map.90 = (f32[248,1024]{1,0:T(8,128)}, f32[248,1024]{1,0:T(8,128)}, f32[248,1024]{1,0:T(8,128)}, f32[24,1024]{1,0:T(8,128)}, f32[8,1024]{1,0:T(8,128)}) custom-call(f32[256,1024]{1,0:T(8,128)} %get-tuple-element.41.rhs_ref, f32[8,256,128]{2,1,0:T(8,128)} %get-tuple-element.42.dia_ref, f32[128,1024]{1,0:T(8,128)} %copy-done.18, ...), custom_call_target="tpu_custom_call" | custom-call | flops 10485760 | bytes 7864320 | tf_op jit(solution)/shard_map/pallas_call | solution.py:351
  157.2 9.9 %all-gather.1 = f32[64,1024]{1,0:T(8,128)S(1)} all-gather(f32[8,1024]{1,0:T(8,128)} %get-tuple-element.43), channel_id=3, replica_groups=mesh['xy'=8,'gz'=4] {'xy'}, dimensions={0}, use_global_device_ids=true | all-gather | bytes 294912 | tf_op jit(solution)/shard_map/all_gather | solution.py:445
  167.9 4.8 %shard_map.91 = (f32[1024,256]{1,0:T(8,128)}, f32[1024,256]{1,0:T(8,128)}) custom-call(s32[1]{0:T(128)} %bitcast.me_ref, f32[8,8,1024]{2,1,0:T(8,128)} %bitcast.54, f32[248,1024]{1,0:T(8,128)} %get-tuple-element.44.c_ref, f32[248,1024]{1,0:T(8,128)} %get-tuple-element.45.g_ref, f32[248,1024]{1,0:T(8,128)} %get-tuple-element.46.f_ref, ...), custom_call_target="tpu_custom_call" | custom-call | flops 10485760 | bytes 7864320 | tf_op jit(solution)/shard_map/pallas_call | solution.py:351
  172.7 19.7 %all_to_all.25 = f32[8,128,256]{2,1,0:T(8,128)} all-to-all(f32[8,128,256]{2,1,0:T(8,128)} %bitcast.59), channel_id=1, replica_groups=mesh['xy'=8,'gz'=4] {'xy'}, dimensions={0} | all-to-all | bytes 2097152 | tf_op jit(solution)/shard_map/all_to_all | solution.py:424
  192.5 18.5 %all_to_all.26 = f32[8,128,256]{2,1,0:T(8,128)} all-to-all(f32[8,128,256]{2,1,0:T(8,128)S(1)} %bitcast.56), channel_id=1, replica_groups=mesh['xy'=8,'gz'=4] {'xy'}, dimensions={0} | all-to-all | bytes 2097152 | tf_op jit(solution)/shard_map/all_to_all | solution.py:424
  210.9 18.5 %all_to_all.27 = f32[8,128,256]{2,1,0:T(8,128)} all-to-all(f32[8,128,256]{2,1,0:T(8,128)S(1)} %bitcast.58), channel_id=1, replica_groups=mesh['xy'=8,'gz'=4] {'xy'}, dimensions={0} | all-to-all | bytes 2097152 | tf_op jit(solution)/shard_map/all_to_all | solution.py:424
  246.5 13.1 %all-to-all-done.4 = f32[8,256,256]{2,1,0:T(8,128)S(1)} async-done(((f32[8,256,256]{2,1,0:T(8,128)}), f32[8,256,256]{2,1,0:T(8,128)S(1)}, u32[]{:S(2)}, u32[]{:S(2)}) %all-to-all-start.4) | async-done | bytes 2097184 | tf_op jit(solution)/shard_map/all_to_all | solution.py:424
  (87 shorter events, 65.9 us)
Async XLA Ops:
  0.6 16.2 %copy-start.2 = (f32[1,256,2048]{2,1,0:T(8,128)S(1)}, f32[1,256,2048]{2,1,0:T(8,128)}, u32[]{:S(2)}) copy-start(f32[1,256,2048]{2,1,0:T(8,128)} %param.8) | copy-start | bytes 6291460
  2.6 16.3 %copy-start.4 = (f32[128,2048]{1,0:T(8,128)}, f32[128,2048]{1,0:T(8,128)S(1)}, u32[]{:S(2)}) copy-start(f32[128,2048]{1,0:T(8,128)S(1)} %get-tuple-element.61.e_ref) | copy-start | bytes 3145732
  2.6 16.3 %copy-start.5 = (f32[128,2048]{1,0:T(8,128)}, f32[128,2048]{1,0:T(8,128)S(1)}, u32[]{:S(2)}) copy-start(f32[128,2048]{1,0:T(8,128)S(1)} %get-tuple-element.62.e_ref) | copy-start | bytes 3145732
  2.6 28.5 %collective-permute-start.3 = (f32[128,2048]{1,0:T(8,128)S(1)}, f32[128,2048]{1,0:T(8,128)S(1)}, u32[]{:S(2)}, u32[]{:S(2)}) collective-permute-start(f32[128,2048]{1,0:T(8,128)S(1)} %get-tuple-element.62.e_ref), channel_id=1, source_target_pairs={{0,1},{1,2},{2,3},{4,5},{5,6},{6,7},{8,9},{9,10},{10,11},{12,13},{... | collective-permute-start | bytes 3145736 | tf_op jit(solution)/shard_map/ppermute | solution.py:19
  7.6 28.0 %collective-permute-start.4 = (f32[128,2048]{1,0:T(8,128)S(1)}, f32[128,2048]{1,0:T(8,128)S(1)}, u32[]{:S(2)}, u32[]{:S(2)}) collective-permute-start(f32[128,2048]{1,0:T(8,128)S(1)} %get-tuple-element.62.e_ref), channel_id=1, source_target_pairs={{1,0},{2,1},{3,2},{5,4},{6,5},{7,6},{9,8},{10,9},{11,10},{13,12},{... | collective-permute-start | bytes 3145736 | tf_op jit(solution)/shard_map/ppermute | solution.py:19
  8.9 44.7 %collective-permute-start.5 = (f32[128,2048]{1,0:T(8,128)S(1)}, f32[128,2048]{1,0:T(8,128)S(1)}, u32[]{:S(2)}, u32[]{:S(2)}) collective-permute-start(f32[128,2048]{1,0:T(8,128)S(1)} %get-tuple-element.61.e_ref), channel_id=1, source_target_pairs={{0,1},{1,2},{2,3},{4,5},{5,6},{6,7},{8,9},{9,10},{10,11},{12,13},{... | collective-permute-start | bytes 3145736 | tf_op jit(solution)/shard_map/ppermute | solution.py:19
  13.5 44.5 %collective-permute-start.6 = (f32[128,2048]{1,0:T(8,128)S(1)}, f32[128,2048]{1,0:T(8,128)S(1)}, u32[]{:S(2)}, u32[]{:S(2)}) collective-permute-start(f32[128,2048]{1,0:T(8,128)S(1)} %get-tuple-element.61.e_ref), channel_id=1, source_target_pairs={{1,0},{2,1},{3,2},{5,4},{6,5},{7,6},{9,8},{10,9},{11,10},{13,12},{... | collective-permute-start | bytes 3145736 | tf_op jit(solution)/shard_map/ppermute | solution.py:19
  15.4 5.0 %collective-permute-start.2 = (f32[1,2048]{1,0:T(1,128)S(1)}, f32[1,2048]{1,0:T(1,128)S(1)}, u32[]{:S(2)}, u32[]{:S(2)}) collective-permute-start(f32[1,2048]{1,0:T(1,128)S(1)} %get-tuple-element.58), channel_id=1, source_target_pairs={{0,4},{4,8},{8,12},{12,16},{16,20},{20,24},{24,28},{1,5},{5,9},{9,... | collective-permute-start | bytes 24584 | tf_op jit(solution)/shard_map/ppermute | solution.py:19
  20.4 15.2 %copy-start.22 = (f32[1,2048]{1,0:T(1,128)}, f32[1,2048]{1,0:T(1,128)S(1)}, u32[]{:S(2)}) copy-start(f32[1,2048]{1,0:T(1,128)S(1)} %collective-permute-done.2.hx_edge_ref) | copy-start | bytes 24580
  45.1 47.1 %collective-permute-start.7 = (f32[128,1024]{1,0:T(8,128)}, f32[128,1024]{1,0:T(8,128)S(1)}, u32[]{:S(2)}, u32[]{:S(2)}) collective-permute-start(f32[128,1024]{1,0:T(8,128)} %get-tuple-element.28.rest_0_), channel_id=1, source_target_pairs={{0,1},{1,2},{2,3},{4,5},{5,6},{6,7},{8,9},{9,10},{10,11},{12,13},{... | collective-permute-start | bytes 1572872 | tf_op jit(solution)/shard_map/ppermute | solution.py:19
  48.5 43.6 %collective-permute-start.9 = (f32[128,1024]{1,0:T(8,128)}, f32[128,1024]{1,0:T(8,128)S(1)}, u32[]{:S(2)}, u32[]{:S(2)}) collective-permute-start(f32[128,1024]{1,0:T(8,128)} %get-tuple-element.28.rest_0_), channel_id=1, source_target_pairs={{1,0},{2,1},{3,2},{5,4},{6,5},{7,6},{9,8},{10,9},{11,10},{13,12},{... | collective-permute-start | bytes 1572872 | tf_op jit(solution)/shard_map/ppermute | solution.py:19
  67.5 24.7 %collective-permute-start.10 = (f32[128,1024]{1,0:T(8,128)}, f32[128,1024]{1,0:T(8,128)S(1)}, u32[]{:S(2)}, u32[]{:S(2)}) collective-permute-start(f32[128,1024]{1,0:T(8,128)} %get-tuple-element.30.rest_2_), channel_id=1, source_target_pairs={{1,0},{2,1},{3,2},{5,4},{6,5},{7,6},{9,8},{10,9},{11,10},{13,12},{... | collective-permute-start | bytes 1572872 | tf_op jit(solution)/shard_map/ppermute | solution.py:19
  68.8 23.4 %collective-permute-start.8 = (f32[128,1024]{1,0:T(8,128)}, f32[128,1024]{1,0:T(8,128)S(1)}, u32[]{:S(2)}, u32[]{:S(2)}) collective-permute-start(f32[128,1024]{1,0:T(8,128)} %get-tuple-element.30.rest_2_), channel_id=1, source_target_pairs={{0,1},{1,2},{2,3},{4,5},{5,6},{6,7},{8,9},{9,10},{10,11},{12,13},{... | collective-permute-start | bytes 1572872 | tf_op jit(solution)/shard_map/ppermute | solution.py:19
  74.3 2.1 collective-permute-start
  76.4 4.7 %collective-permute-start.1 = (f32[1,2048]{1,0:T(1,128)S(1)}, f32[1,2048]{1,0:T(1,128)S(1)}, u32[]{:S(2)}, u32[]{:S(2)}) collective-permute-start(f32[1,2048]{1,0:T(1,128)S(1)} %get-tuple-element.63), channel_id=1, source_target_pairs={{4,0},{8,4},{12,8},{16,12},{20,16},{24,20},{28,24},{5,1},{9,5},{13... | collective-permute-start | bytes 24584 | tf_op jit(solution)/shard_map/ppermute | solution.py:19
  116.5 56.2 %all-to-all-start.2 = ((f32[8,128,256]{2,1,0:T(8,128)}), f32[8,128,256]{2,1,0:T(8,128)S(1)}, u32[]{:S(2)}, u32[]{:S(2)}) async-start(f32[8,128,256]{2,1,0:T(8,128)} %bitcast.57), calls=%async_computation.2 | async-start | bytes 2097152 | tf_op jit(solution)/shard_map/all_to_all | solution.py:424
  120.2 15.7 %collective-permute-start.11 = (f32[128,1024]{1,0:T(8,128)S(1)}, f32[128,1024]{1,0:T(8,128)S(1)}, u32[]{:S(2)}, u32[]{:S(2)}) collective-permute-start(f32[128,1024]{1,0:T(8,128)S(1)} %copy-done.12), channel_id=1, source_target_pairs={{0,1},{1,2},{2,3},{4,5},{5,6},{6,7},{8,9},{9,10},{10,11},{12,13},{... | collective-permute-start | bytes 1572872 | tf_op jit(solution)/shard_map/ppermute | solution.py:19
  123.6 16.7 %collective-permute-start.13 = (f32[128,1024]{1,0:T(8,128)S(1)}, f32[128,1024]{1,0:T(8,128)S(1)}, u32[]{:S(2)}, u32[]{:S(2)}) collective-permute-start(f32[128,1024]{1,0:T(8,128)S(1)} %copy-done.12), channel_id=1, source_target_pairs={{1,0},{2,1},{3,2},{5,4},{6,5},{7,6},{9,8},{10,9},{11,10},{13,12},{... | collective-permute-start | bytes 1572872 | tf_op jit(solution)/shard_map/ppermute | solution.py:19
  125.0 21.6 %collective-permute-start.12 = (f32[128,1024]{1,0:T(8,128)S(1)}, f32[128,1024]{1,0:T(8,128)S(1)}, u32[]{:S(2)}, u32[]{:S(2)}) collective-permute-start(f32[128,1024]{1,0:T(8,128)S(1)} %copy-done.13), channel_id=1, source_target_pairs={{0,1},{1,2},{2,3},{4,5},{5,6},{6,7},{8,9},{9,10},{10,11},{12,13},{... | collective-permute-start | bytes 1572872 | tf_op jit(solution)/shard_map/ppermute | solution.py:19
  129.5 21.1 %collective-permute-start.14 = (f32[128,1024]{1,0:T(8,128)S(1)}, f32[128,1024]{1,0:T(8,128)S(1)}, u32[]{:S(2)}, u32[]{:S(2)}) collective-permute-start(f32[128,1024]{1,0:T(8,128)S(1)} %copy-done.13), channel_id=1, source_target_pairs={{1,0},{2,1},{3,2},{5,4},{6,5},{7,6},{9,8},{10,9},{11,10},{13,12},{... | collective-permute-start | bytes 1572872 | tf_op jit(solution)/shard_map/ppermute | solution.py:19
  135.9 14.8 %copy-start.18 = (f32[128,1024]{1,0:T(8,128)}, f32[128,1024]{1,0:T(8,128)S(1)}, u32[]{:S(2)}) copy-start(f32[128,1024]{1,0:T(8,128)S(1)} %collective-permute-done.11.rest_0_) | copy-start | bytes 1572868
  172.7 19.8 %copy-start.6 = (f32[1024,256]{1,0:T(8,128)S(1)}, f32[1024,256]{1,0:T(8,128)}, u32[]{:S(2)}) copy-start(f32[1024,256]{1,0:T(8,128)} %get-tuple-element.40) | copy-start | bytes 3145732
  172.7 38.2 %copy-start.7 = (f32[1024,256]{1,0:T(8,128)S(1)}, f32[1024,256]{1,0:T(8,128)}, u32[]{:S(2)}) copy-start(f32[1024,256]{1,0:T(8,128)} %get-tuple-element.49) | copy-start | bytes 3145732
  229.4 30.2 %all-to-all-start.4 = ((f32[8,256,256]{2,1,0:T(8,128)}), f32[8,256,256]{2,1,0:T(8,128)S(1)}, u32[]{:S(2)}, u32[]{:S(2)}) async-start(f32[8,256,256]{2,1,0:T(8,128)} %bitcast.53), calls=%async_computation.4 | async-start | bytes 4194304 | tf_op jit(solution)/shard_map/all_to_all | solution.py:424
  (18 other events, 68.4 us)
where the time goes:
time: 266 us; the launch traced here: 265 us
  blocking collectives  78.2 us (29%)
  waiting for transfers between devices  60.4 us (23%)
  Pallas kernels  48.4 us (18%)
  starting transfers between devices  44.8 us (17%)
  local copies, waits for them, and re-layouts  29.2 us (11%)
  other arithmetic  2.86 us (1%)
    all_to_all x3, blocking collectives, exchanged(): lax.all_to_all(values.reshape(count, size, rows), 'xy', split_axis=0, con...  56.7 us
    pallas_call x7, Pallas kernels, called(): pl.pallas_call(kernel, out_shape=[jax.ShapeDtypeStruct(shape, jnp.float32...  48.4 us
    ppermute x15, waiting for transfers between devices, passed_along(): lax.ppermute(value, axis, [(source, source + steps) for source in range(i...  47.3 us
    ppermute x15, starting transfers between devices, passed_along(): lax.ppermute(value, axis, [(source, source + steps) for source in range(i...  37.6 us
    all_gather x2, blocking collectives, local(): everyone = jnp.swapaxes(lax.all_gather(firsts[4], 'xy'), 0, 1)  21.5 us
    all_to_all x2, waiting for transfers between devices, exchanged(): lax.all_to_all(values.reshape(count, size, rows), 'xy', split_axis=0, con...  13.1 us
    reshape x3, local copies, waits for them, and re-layouts, joined(): jnp.transpose(moved, (1, 0, 2)).reshape(1, moved.shape[1], count * rows)  8.19 us
    transpose x3, local copies, waits for them, and re-layouts, joined(): jnp.transpose(moved, (1, 0, 2)).reshape(1, moved.shape[1], count * rows)  7.65 us
  transfers between devices with their start and end apart: 17, of which 11 were waited for; matrix products, arithmetic and copies ran while one was open for 7% of the time, Pallas kernels for 14%

commit v1 on v0

--- a/solution.py
+++ b/solution.py
@@ -361,6 +361,105 @@
     )(*operands)
 
 
+def greet(count, me):
+    barrier = pltpu.get_barrier_semaphore()
+    for step in range(1, count):
+        pl.semaphore_signal(
+            barrier, inc=1, device_id={"xy": lax.rem(me + step, count)},
+            device_id_type=pl.DeviceIdType.MESH,
+        )
+    pl.semaphore_wait(barrier, count - 1)
+
+
+def spread_kernel(count, arrays, *refs):
+    sources, outs = refs[:arrays], refs[arrays:2 * arrays]
+    send_sems, recv_sems, own_sems = refs[2 * arrays:]
+    me = lax.axis_index("xy")
+    height, width = outs[0].shape[0], sources[0].shape[1]
+
+    def rows_of(device):
+        return pl.ds(pl.multiple_of(device * height, height), height)
+
+    def columns_of(device):
+        return pl.ds(pl.multiple_of(device * width, width), width)
+
+    greet(count, me)
+    owns, copies = [], []
+    for step in range(1, count):
+        peer = lax.rem(me + step, count)
+        for k in range(arrays):
+            copy = pltpu.make_async_remote_copy(
+                src_ref=sources[k].at[rows_of(peer), :],
+                dst_ref=outs[k].at[:, columns_of(me)],
+                send_sem=send_sems.at[k, step - 1],
+                recv_sem=recv_sems.at[k, step - 1],
+                device_id={"xy": peer},
+                device_id_type=pl.DeviceIdType.MESH,
+            )
+            copy.start()
+            copies.append(copy)
+    for k in range(arrays):
+        own = pltpu.make_async_copy(
+            sources[k].at[rows_of(me), :], outs[k].at[:, columns_of(me)], own_sems.at[k]
+        )
+        own.start()
+        owns.append(own)
+    for own in owns:
+        own.wait()
+    for copy in copies:
+        copy.wait()
+
+
+def spread(values, count, number):
+    columns, rows = values[0].shape
+    anywhere = pl.BlockSpec(memory_space=pl.ANY)
+    arrays = len(values)
+    sems = pltpu.SemaphoreType.DMA((arrays, count - 1))
+    return pl.pallas_call(
+        functools.partial(spread_kernel, count, arrays),
+        out_shape=[jax.ShapeDtypeStruct((columns // count, rows * count), jnp.float32)] * arrays,
+        in_specs=[anywhere] * arrays,
+        out_specs=[anywhere] * arrays,
+        scratch_shapes=[sems, sems, pltpu.SemaphoreType.DMA((arrays,))],
+        compiler_params=pltpu.CompilerParams(collective_id=number, has_side_effects=True),
+        cost_estimate=pl.CostEstimate(
+            flops=0, bytes_accessed=32 * arrays * rows * columns, transcendentals=0
+        ),
+    )(*values)
+
+
+def gather_kernel(count, source, out, send_sems, recv_sems):
+    me = lax.axis_index("xy")
+    greet(count, me)
+    copies = []
+    for step in range(1, count):
+        copy = pltpu.make_async_remote_copy(
+            src_ref=source,
+            dst_ref=out.at[me],
+            send_sem=send_sems.at[step - 1],
+            recv_sem=recv_sems.at[step - 1],
+            device_id={"xy": lax.rem(me + step, count)},
+            device_id_type=pl.DeviceIdType.MESH,
+        )
+        copy.start()
+        copies.append(copy)
+    out[me] = source[...]
+    for copy in copies:
+        copy.wait()
+
+
+def gathered(value, count, number):
+    sems = pltpu.SemaphoreType.DMA((count - 1,))
+    return pl.pallas_call(
+        functools.partial(gather_kernel, count),
+        out_shape=jax.ShapeDtypeStruct((count,) + value.shape, jnp.float32),
+        in_specs=[in_vmem],
+        out_specs=in_vmem,
+        scratch_shapes=[sems, sems],
+        compiler_params=pltpu.CompilerParams(collective_id=number, has_side_effects=True),
+    )(value)
+
+
 def local(
     electric, magnetic_first, magnetic_second, region, permittivity_table, conductivity_table
 ):
@@ -369,7 +468,7 @@
     _, rows, columns = electric.shape
     width = columns // count
     pieces = 2 if rows % 256 == 0 else 1
-    parts = 2 if width == 256 else 1
+    parts = 1
     piece_rows = rows // pieces
     part_columns = columns // parts
     runs = 8
@@ -429,33 +528,36 @@
     def joined(moved):
         return jnp.transpose(moved, (1, 0, 2)).reshape(1, moved.shape[1], count * rows)
 
-    full_hy = joined(exchanged(full_hy_t, width))
-    pairs = []
-    for c in range(parts):
-        length = rows // runs
-        kept = ((length - 1) * runs, part_columns)
-        firsts = called(
-            functools.partial(y_first_kernel, pieces, runs),
-            [kept] * 3 + [(3 * runs, part_columns), (8, part_columns)],
-            [(part_columns // 128, rows, 128)],
-            [in_vmem] * (2 + 2 * pieces),
-            rows * part_columns,
-            (right_sides[c], diagonals[c], *half_up[c], *half_down[c]),
-        )
-        everyone = jnp.swapaxes(lax.all_gather(firsts[4], "xy"), 0, 1)
-        seconds = called(
-            functools.partial(y_second_kernel, count, runs),
-            [(part_columns, rows)] * 2,
-            [(part_columns // 128, rows, 128), (rows, part_columns), (runs, part_columns)],
-            [in_smem] + [in_vmem] * 6,
-            rows * part_columns,
-            (me_value, everyone, *firsts[:4], half_hx[c]),
-        )
-        pairs.append([exchanged(v, width // parts) for v in seconds])
-    full_e, full_hx = (
-        joined(jnp.concatenate([pair[q] for pair in pairs], axis=1)) for q in range(2)
-    )
-    return (full_e, full_hx, full_hy)
+    by_kernel = rows % 128 == 0 and width % 8 == 0 and 1 < count <= 16
+    if by_kernel:
+        full_hy, = spread([full_hy_t], count, 0)
+        full_hy, right_side = lax.optimization_barrier((full_hy, right_sides[0]))
+    else:
+        full_hy, right_side = joined(exchanged(full_hy_t, width)), right_sides[0]
+    length = rows // runs
+    kept = ((length - 1) * runs, columns)
+    firsts = called(
+        functools.partial(y_first_kernel, pieces, runs),
+        [kept] * 3 + [(3 * runs, columns), (8, columns)],
+        [(columns // 128, rows, 128)],
+        [in_vmem] * (2 + 2 * pieces),
+        rows * columns,
+        (right_side, diagonals[0], *half_up[0], *half_down[0]),
+    )
+    everyone = gathered(firsts[4], count, 1) if by_kernel else lax.all_gather(firsts[4], "xy")
+    seconds = called(
+        functools.partial(y_second_kernel, count, runs),
+        [(columns, rows)] * 2,
+        [(columns // 128, rows, 128), (rows, columns), (runs, columns)],
+        [in_smem] + [in_vmem] * 6,
+        rows * columns,
+        (me_value, jnp.swapaxes(everyone, 0, 1), *firsts[:4], half_hx[0]),
+    )
+    if by_kernel:
+        full_e, full_hx = spread(seconds, count, 2)
+    else:
+        full_e, full_hx = (joined(exchanged(v, width)) for v in seconds)
+    return tuple(v.reshape(1, width, count * rows) for v in (full_e, full_hx, full_hy))
 
 
 def solution(mesh):

time: 266 us -> 208 us (0.78)
  Pallas kernels: 48.4 us -> 131 us
  blocking collectives: 78.2 us -> 0 us
  waiting for transfers between devices: 60.4 us -> 20.9 us
  starting transfers between devices: 44.8 us -> 33.9 us
  local copies, waits for them, and re-layouts: 29.2 us -> 20.3 us
  other arithmetic: 2.86 us -> 0 us
    pallas_call x0 -> x3, Pallas kernels: none -> 86.2 us  [the longest x2 75.3 us: spread(): pl.pallas_call(functools.partial(spread_kernel, count, arrays), out_shape...]
    all_to_all x3 -> x0, blocking collectives: 56.7 us -> none  [exchanged(): lax.all_to_all(values.reshape(count, size, rows), 'xy', split_axis=0, con...]
    ppermute x15 -> x11, waiting for transfers between devices: 47.3 us -> 20.9 us  [passed_along(): lax.ppermute(value, axis, [(source, source + steps) for source in range(i...]
    all_gather x2 -> x0, blocking collectives: 21.5 us -> none  [local(): everyone = jnp.swapaxes(lax.all_gather(firsts[4], 'xy'), 0, 1)]
    all_to_all x2 -> x0, waiting for transfers between devices: 13.1 us -> none  [exchanged(): lax.all_to_all(values.reshape(count, size, rows), 'xy', split_axis=0, con...]
    reshape x3 -> x0, local copies, waits for them, and re-layouts: 8.19 us -> none  [joined(): jnp.transpose(moved, (1, 0, 2)).reshape(1, moved.shape[1], count * rows)]
    transpose x3 -> x0, local copies, waits for them, and re-layouts: 7.65 us -> none  [joined(): jnp.transpose(moved, (1, 0, 2)).reshape(1, moved.shape[1], count * rows)]
    all_to_all x2 -> x0, starting transfers between devices: 7.29 us -> none  [exchanged(): lax.all_to_all(values.reshape(count, size, rows), 'xy', split_axis=0, con...]
  transfers between devices with their start and end apart: 17 -> 11, of which waited for: 11 -> 6; matrix products, arithmetic and copies ran while one was open for 7% -> 2% of each run, Pallas kernels for 14% -> 26%
where the time goes in v1:
time: 208 us; the launch traced here: 207 us
  Pallas kernels  131 us (63%)
  starting transfers between devices  33.9 us (16%)
  waiting for transfers between devices  20.9 us (10%)
  local copies, waits for them, and re-layouts  20.3 us (10%)
    pallas_call x2, Pallas kernels, spread(): pl.pallas_call(functools.partial(spread_kernel, count, arrays), out_shape...  75.3 us
    pallas_call x5, Pallas kernels, called(): pl.pallas_call(kernel, out_shape=[jax.ShapeDtypeStruct(shape, jnp.float32...  45.2 us
    ppermute x11, starting transfers between devices, passed_along(): lax.ppermute(value, axis, [(source, source + steps) for source in range(i...  33.9 us
    ppermute x11, waiting for transfers between devices, passed_along(): lax.ppermute(value, axis, [(source, source + steps) for source in range(i...  20.9 us
    unnamed x37, local copies, waits for them, and re-layouts  11.1 us
    pallas_call x1, Pallas kernels, gathered(): pl.pallas_call(functools.partial(gather_kernel, count), out_shape=jax.Sha...  10.9 us
  transfers between devices with their start and end apart: 11, of which 6 were waited for; matrix products, arithmetic and copies ran while one was open for 2% of the time, Pallas kernels for 26%

profile of v1, /device:TPU:0, one launch (start us, length us, event | category | flops | bytes accessed | tf_op | source)
XLA Modules:
  0.0 207.3 jit_solution(14000163666299287686)
XLA Ops:
  0.7 1.9 slice_bitcast_fusion.3
  3.9 5.6 %collective-permute-start.5 = (f32[128,2048]{1,0:T(8,128)S(1)}, f32[128,2048]{1,0:T(8,128)S(1)}, u32[]{:S(2)}, u32[]{:S(2)}) collective-permute-start(f32[128,2048]{1,0:T(8,128)S(1)} %get-tuple-element.41.e_ref), channel_id=1, source_target_pairs={{0,1},{1,2},{2,3},{4,5},{5,6},{6,7},{8,9},{9,10},{10,11},{12,13},{... | collective-permute-start | bytes 3145736 | tf_op jit(solution)/shard_map/ppermute | solution.py:19
  10.8 4.6 %collective-permute-start.3 = (f32[128,2048]{1,0:T(8,128)S(1)}, f32[128,2048]{1,0:T(8,128)S(1)}, u32[]{:S(2)}, u32[]{:S(2)}) collective-permute-start(f32[128,2048]{1,0:T(8,128)S(1)} %get-tuple-element.42.e_ref), channel_id=1, source_target_pairs={{0,1},{1,2},{2,3},{4,5},{5,6},{6,7},{8,9},{9,10},{10,11},{12,13},{... | collective-permute-start | bytes 3145736 | tf_op jit(solution)/shard_map/ppermute | solution.py:19
  16.0 1.4 collective-permute-start.2
  17.5 2.1 %slice_bitcast_fusion.1 = (f32[128,2048]{1,0:T(8,128)}, f32[128,2048]{1,0:T(8,128)}, f32[128,2048]{1,0:T(8,128)}, f32[128,2048]{1,0:T(8,128)}) fusion(f32[1,256,2048]{2,1,0:T(8,128)S(1)} %copy-done.2, f32[1,256,2048]{2,1,0:T(8,128)S(1)} %copy-done), kind=kLoop, calls=%fused_computation.1 | loop fusion | bytes 8388608 | tf_op jit(solution)/shard_map/slice | solution.py:500
  19.6 1.5 slice_bitcast_fusion
  21.1 10.4 %collective-permute-done.6.down_ref = f32[128,2048]{1,0:T(8,128)S(1)} collective-permute-done((f32[128,2048]{1,0:T(8,128)S(1)}, f32[128,2048]{1,0:T(8,128)S(1)}, u32[]{:S(2)}, u32[]{:S(2)}) %collective-permute-start.6) | collective-permute-done | bytes 1048608 | tf_op jit(solution)/shard_map/ppermute | solution.py:19
  31.5 1.5 collective-permute-done.5.up_ref
  33.9 8.5 %shard_map.86.rest_1_ = f32[128,2048]{1,0:T(8,128)} custom-call(f32[128,2048]{1,0:T(8,128)} %copy-done.5, f32[128,2048]{1,0:T(8,128)} %copy-done.10, f32[128,2048]{1,0:T(8,128)} %copy-done.9, f32[128,2048]{1,0:T(8,128)} %get-tuple-element.46.hx_ref, f32[1,2048]{1,0:T(1,128)} %get-tuple-element.37.hx_edge_ref, f32[128,2048]{1,0:T(8,128)} %get-tuple-element.35.hy_ref, ...), custom_call_target="tpu_custom_call" | custom-call | flops 10485760 | bytes 7864320 | tf_op jit(solution)/shard_map/pallas_call | solution.py:351
  43.7 5.1 %collective-permute-start.8 = (f32[128,2048]{1,0:T(8,128)}, f32[128,2048]{1,0:T(8,128)S(1)}, u32[]{:S(2)}, u32[]{:S(2)}) collective-permute-start(f32[128,2048]{1,0:T(8,128)} %shard_map.86.rest_1_), channel_id=1, source_target_pairs={{0,1},{1,2},{2,3},{4,5},{5,6},{6,7},{8,9},{9,10},{10,11},{12,13},{... | collective-permute-start | bytes 3145736 | tf_op jit(solution)/shard_map/ppermute | solution.py:19
  48.8 5.1 %collective-permute-done.4.down_ref = f32[128,2048]{1,0:T(8,128)S(1)} collective-permute-done((f32[128,2048]{1,0:T(8,128)S(1)}, f32[128,2048]{1,0:T(8,128)S(1)}, u32[]{:S(2)}, u32[]{:S(2)}) %collective-permute-start.4) | collective-permute-done | bytes 1048608 | tf_op jit(solution)/shard_map/ppermute | solution.py:19
  53.9 1.5 collective-permute-done.3.up_ref
  56.4 8.5 %shard_map.85.rest_0_ = f32[128,2048]{1,0:T(8,128)} custom-call(f32[128,2048]{1,0:T(8,128)} %copy-done.4, f32[128,2048]{1,0:T(8,128)} %copy-done.8, f32[128,2048]{1,0:T(8,128)} %copy-done.7, f32[128,2048]{1,0:T(8,128)} %get-tuple-element.45.hx_ref, f32[1,2048]{1,0:T(1,128)} %copy-done.14, f32[128,2048]{1,0:T(8,128)} %get-tuple-element.36.hy_ref, ...), custom_call_target="tpu_custom_call" | custom-call | flops 10485760 | bytes 7864320 | tf_op jit(solution)/shard_map/pallas_call | solution.py:351
  66.2 6.1 %collective-permute-start.7 = (f32[128,2048]{1,0:T(8,128)}, f32[128,2048]{1,0:T(8,128)}, u32[]{:S(2)}, u32[]{:S(2)}) collective-permute-start(f32[128,2048]{1,0:T(8,128)} %shard_map.85.rest_0_), channel_id=1, source_target_pairs={{0,1},{1,2},{2,3},{4,5},{5,6},{6,7},{8,9},{9,10},{10,11},{12,13},{... | collective-permute-start | bytes 3145736 | tf_op jit(solution)/shard_map/ppermute | solution.py:19
  74.4 1.8 collective-permute-done.1.e_after_ref
  76.2 4.6 %collective-permute-start = (f32[1,2048]{1,0:T(1,128)S(1)}, f32[1,2048]{1,0:T(1,128)S(1)}, u32[]{:S(2)}, u32[]{:S(2)}) collective-permute-start(f32[1,2048]{1,0:T(1,128)S(1)} %get-tuple-element.44), channel_id=1, source_target_pairs={{0,4},{4,8},{8,12},{12,16},{16,20},{20,24},{24,28},{1,5},{5,9},{9,... | collective-permute-start | bytes 24584 | tf_op jit(solution)/shard_map/ppermute | solution.py:19
  82.1 10.4 %shard_map.87 = (f32[256,2048]{1,0:T(8,128)}, f32[16,256,128]{2,1,0:T(8,128)}, f32[256,2048]{1,0:T(8,128)}, f32[2048,256]{1,0:T(8,128)}) custom-call(s32[1]{0:T(128)} %bitcast.1.first_ref, f32[256,2048]{1,0:T(8,128)} %bitcast.36, f32[256,2048]{1,0:T(8,128)} %bitcast.37, f32[256,2048]{1,0:T(8,128)} %bitcast.39, s32[256,2048]{1,0:T(8,128)} %bitcast.38, ...), custom_call_target="tpu_custom_call" | custom-call | flops 20971520 | bytes 15728640 | tf_op jit(solution)/shard_map/pallas_call | solution.py:351
  92.5 26.6 %shard_map.88 = f32[256,2048]{1,0:T(8,128)} custom-call(f32[2048,256]{1,0:T(8,128)} %get-tuple-element.18.refs_0_), custom_call_target="tpu_custom_call" | custom-call | bytes 16777216 | tf_op jit(solution)/shard_map/pallas_call | solution.py:418
  120.8 9.9 %shard_map.89 = (f32[248,2048]{1,0:T(8,128)}, f32[248,2048]{1,0:T(8,128)}, f32[248,2048]{1,0:T(8,128)}, f32[24,2048]{1,0:T(8,128)}, f32[8,2048]{1,0:T(8,128)}) custom-call(f32[256,2048]{1,0:T(8,128)} %get-tuple-element.20.rhs_ref, f32[16,256,128]{2,1,0:T(8,128)} %get-tuple-element.21.dia_ref, f32[128,2048]{1,0:T(8,128)} %collective-permute-done.7.rest_0_, ...), custom_call_target="tpu_custom_call" | custom-call | flops 20971520 | bytes 15728640 | tf_op jit(solution)/shard_map/pallas_call | solution.py:351
  130.6 10.9 %shard_map.90 = f32[8,8,2048]{2,1,0:T(8,128)} custom-call(f32[8,2048]{1,0:T(8,128)} %get-tuple-element.22.source), custom_call_target="tpu_custom_call" | custom-call | tf_op jit(solution)/shard_map/pallas_call | solution.py:453
  141.5 2.2 %copy.11 = f32[8,8,2048]{2,0,1:T(8,128)} copy(f32[8,8,2048]{2,1,0:T(8,128)} %shard_map.90) | data formatting | bytes 1048576 | tf_op jit(solution)/shard_map/pallas_call | solution.py:453
  143.7 7.8 %shard_map.91 = (f32[2048,256]{1,0:T(8,128)}, f32[2048,256]{1,0:T(8,128)}) custom-call(s32[1]{0:T(128)} %bitcast.me_ref, f32[8,8,2048]{2,1,0:T(8,128)} %bitcast.41, f32[248,2048]{1,0:T(8,128)} %get-tuple-element.23.c_ref, f32[248,2048]{1,0:T(8,128)} %get-tuple-element.24.g_ref, f32[248,2048]{1,0:T(8,128)} %get-tuple-element.25.f_ref, ...), custom_call_target="tpu_custom_call" | custom-call | flops 20971520 | bytes 15728640 | tf_op jit(solution)/shard_map/pallas_call | solution.py:351
  151.6 48.7 %shard_map.92 = (f32[256,2048]{1,0:T(8,128)}, f32[256,2048]{1,0:T(8,128)}) custom-call(f32[2048,256]{1,0:T(8,128)} %get-tuple-element.28.refs_0_, f32[2048,256]{1,0:T(8,128)} %get-tuple-element.29.refs_1_), custom_call_target="tpu_custom_call" | custom-call | bytes 33554432 | tf_op jit(solution)/shard_map/pallas_call | solution.py:418
  200.3 3.3 %copy.15 = f32[1,256,2048]{2,1,0:T(8,128)} copy(f32[1,256,2048]{2,1,0:T(8,128)} %bitcast.43) | data formatting | bytes 4194304
  (49 shorter events, 16.4 us)
Async XLA Ops:
  0.6 14.8 %copy-start = (f32[1,256,2048]{2,1,0:T(8,128)S(1)}, f32[1,256,2048]{2,1,0:T(8,128)}, u32[]{:S(2)}) copy-start(f32[1,256,2048]{2,1,0:T(8,128)} %param.7) | copy-start | bytes 6291460
  0.6 16.8 %copy-start.2 = (f32[1,256,2048]{2,1,0:T(8,128)S(1)}, f32[1,256,2048]{2,1,0:T(8,128)}, u32[]{:S(2)}) copy-start(f32[1,256,2048]{2,1,0:T(8,128)} %param.8) | copy-start | bytes 6291460
  2.5 17.0 %copy-start.4 = (f32[128,2048]{1,0:T(8,128)}, f32[128,2048]{1,0:T(8,128)S(1)}, u32[]{:S(2)}) copy-start(f32[128,2048]{1,0:T(8,128)S(1)} %get-tuple-element.42.e_ref) | copy-start | bytes 3145732
  2.5 17.0 %copy-start.5 = (f32[128,2048]{1,0:T(8,128)}, f32[128,2048]{1,0:T(8,128)S(1)}, u32[]{:S(2)}) copy-start(f32[128,2048]{1,0:T(8,128)S(1)} %get-tuple-element.41.e_ref) | copy-start | bytes 3145732
  2.6 28.9 %collective-permute-start.6 = (f32[128,2048]{1,0:T(8,128)S(1)}, f32[128,2048]{1,0:T(8,128)S(1)}, u32[]{:S(2)}, u32[]{:S(2)}) collective-permute-start(f32[128,2048]{1,0:T(8,128)S(1)} %get-tuple-element.41.e_ref), channel_id=1, source_target_pairs={{1,0},{2,1},{3,2},{5,4},{6,5},{7,6},{9,8},{10,9},{11,10},{13,12},{... | collective-permute-start | bytes 3145736 | tf_op jit(solution)/shard_map/ppermute | solution.py:19
  3.9 29.1 %collective-permute-start.5 = (f32[128,2048]{1,0:T(8,128)S(1)}, f32[128,2048]{1,0:T(8,128)S(1)}, u32[]{:S(2)}, u32[]{:S(2)}) collective-permute-start(f32[128,2048]{1,0:T(8,128)S(1)} %get-tuple-element.41.e_ref), channel_id=1, source_target_pairs={{0,1},{1,2},{2,3},{4,5},{5,6},{6,7},{8,9},{9,10},{10,11},{12,13},{... | collective-permute-start | bytes 3145736 | tf_op jit(solution)/shard_map/ppermute | solution.py:19
  9.5 44.5 %collective-permute-start.4 = (f32[128,2048]{1,0:T(8,128)S(1)}, f32[128,2048]{1,0:T(8,128)S(1)}, u32[]{:S(2)}, u32[]{:S(2)}) collective-permute-start(f32[128,2048]{1,0:T(8,128)S(1)} %get-tuple-element.42.e_ref), channel_id=1, source_target_pairs={{1,0},{2,1},{3,2},{5,4},{6,5},{7,6},{9,8},{10,9},{11,10},{13,12},{... | collective-permute-start | bytes 3145736 | tf_op jit(solution)/shard_map/ppermute | solution.py:19
  10.8 44.7 %collective-permute-start.3 = (f32[128,2048]{1,0:T(8,128)S(1)}, f32[128,2048]{1,0:T(8,128)S(1)}, u32[]{:S(2)}, u32[]{:S(2)}) collective-permute-start(f32[128,2048]{1,0:T(8,128)S(1)} %get-tuple-element.42.e_ref), channel_id=1, source_target_pairs={{0,1},{1,2},{2,3},{4,5},{5,6},{6,7},{8,9},{9,10},{10,11},{12,13},{... | collective-permute-start | bytes 3145736 | tf_op jit(solution)/shard_map/ppermute | solution.py:19
  16.0 3.5 %copy-start.1 = (s32[1,256,2048]{2,1,0:T(8,128)S(1)}, s32[1,256,2048]{2,1,0:T(8,128)}, u32[]{:S(2)}) copy-start(s32[1,256,2048]{2,1,0:T(8,128)} %param.9) | copy-start | bytes 6291460
  16.0 32.8 %collective-permute-start.2 = (f32[1,2048]{1,0:T(1,128)S(1)}, f32[1,2048]{1,0:T(1,128)S(1)}, u32[]{:S(2)}, u32[]{:S(2)}) collective-permute-start(f32[1,2048]{1,0:T(1,128)S(1)} %get-tuple-element.38), channel_id=1, source_target_pairs={{0,4},{4,8},{8,12},{12,16},{16,20},{20,24},{24,28},{1,5},{5,9},{9,... | collective-permute-start | bytes 24584 | tf_op jit(solution)/shard_map/ppermute | solution.py:19
  31.5 1.5 copy-start.9
  42.4 76.7 %collective-permute-start.10 = (f32[128,2048]{1,0:T(8,128)}, f32[128,2048]{1,0:T(8,128)S(1)}, u32[]{:S(2)}, u32[]{:S(2)}) collective-permute-start(f32[128,2048]{1,0:T(8,128)} %shard_map.86.rest_1_), channel_id=1, source_target_pairs={{1,0},{2,1},{3,2},{5,4},{6,5},{7,6},{9,8},{10,9},{11,10},{13,12},{... | collective-permute-start | bytes 3145736 | tf_op jit(solution)/shard_map/ppermute | solution.py:19
  43.7 75.4 %collective-permute-start.8 = (f32[128,2048]{1,0:T(8,128)}, f32[128,2048]{1,0:T(8,128)S(1)}, u32[]{:S(2)}, u32[]{:S(2)}) collective-permute-start(f32[128,2048]{1,0:T(8,128)} %shard_map.86.rest_1_), channel_id=1, source_target_pairs={{0,1},{1,2},{2,3},{4,5},{5,6},{6,7},{8,9},{9,10},{10,11},{12,13},{... | collective-permute-start | bytes 3145736 | tf_op jit(solution)/shard_map/ppermute | solution.py:19
  48.8 6.6 %copy-start.14 = (f32[1,2048]{1,0:T(1,128)}, f32[1,2048]{1,0:T(1,128)S(1)}, u32[]{:S(2)}) copy-start(f32[1,2048]{1,0:T(1,128)S(1)} %collective-permute-done.2.hx_edge_ref) | copy-start | bytes 24580
  53.9 1.5 copy-start.7
  64.9 54.2 %collective-permute-start.9 = (f32[128,2048]{1,0:T(8,128)}, f32[128,2048]{1,0:T(8,128)S(1)}, u32[]{:S(2)}, u32[]{:S(2)}) collective-permute-start(f32[128,2048]{1,0:T(8,128)} %shard_map.85.rest_0_), channel_id=1, source_target_pairs={{1,0},{2,1},{3,2},{5,4},{6,5},{7,6},{9,8},{10,9},{11,10},{13,12},{... | collective-permute-start | bytes 3145736 | tf_op jit(solution)/shard_map/ppermute | solution.py:19
  66.2 53.0 %collective-permute-start.7 = (f32[128,2048]{1,0:T(8,128)}, f32[128,2048]{1,0:T(8,128)}, u32[]{:S(2)}, u32[]{:S(2)}) collective-permute-start(f32[128,2048]{1,0:T(8,128)} %shard_map.85.rest_0_), channel_id=1, source_target_pairs={{0,1},{1,2},{2,3},{4,5},{5,6},{6,7},{8,9},{9,10},{10,11},{12,13},{... | collective-permute-start | bytes 3145736 | tf_op jit(solution)/shard_map/ppermute | solution.py:19
  73.1 3.1 %collective-permute-start.1 = (f32[1,2048]{1,0:T(1,128)S(1)}, f32[1,2048]{1,0:T(1,128)S(1)}, u32[]{:S(2)}, u32[]{:S(2)}) collective-permute-start(f32[1,2048]{1,0:T(1,128)S(1)} %get-tuple-element.43), channel_id=1, source_target_pairs={{4,0},{8,4},{12,8},{16,12},{20,16},{24,20},{28,24},{5,1},{9,5},{13... | collective-permute-start | bytes 24584 | tf_op jit(solution)/shard_map/ppermute | solution.py:19
  76.2 5.3 %copy-start.15 = (f32[1,2048]{1,0:T(1,128)}, f32[1,2048]{1,0:T(1,128)S(1)}, u32[]{:S(2)}) copy-start(f32[1,2048]{1,0:T(1,128)S(1)} %collective-permute-done.1.e_after_ref) | copy-start | bytes 24580
  76.2 5.3 %collective-permute-start = (f32[1,2048]{1,0:T(1,128)S(1)}, f32[1,2048]{1,0:T(1,128)S(1)}, u32[]{:S(2)}, u32[]{:S(2)}) collective-permute-start(f32[1,2048]{1,0:T(1,128)S(1)} %get-tuple-element.44), channel_id=1, source_target_pairs={{0,4},{4,8},{8,12},{12,16},{16,20},{20,24},{24,28},{1,5},{5,9},{9,... | collective-permute-start | bytes 24584 | tf_op jit(solution)/shard_map/ppermute | solution.py:19
  119.1 1.3 copy-start.12
  119.1 1.6 copy-start.13
  200.3 3.3 %copy-start.6 = (f32[256,2048]{1,0:T(8,128)S(1)}, f32[256,2048]{1,0:T(8,128)}, u32[]{:S(2)}) copy-start(f32[256,2048]{1,0:T(8,128)} %get-tuple-element.31) | copy-start | bytes 6291460
  203.6 2.3 %copy-start.3 = (f32[256,2048]{1,0:T(8,128)S(1)}, f32[256,2048]{1,0:T(8,128)}, u32[]{:S(2)}) copy-start(f32[256,2048]{1,0:T(8,128)} %shard_map.88) | copy-start | bytes 6291460
  (4 other events, 3.5 us)
